TPU v7x, 512 devices: a whole 4x4x16 slice. The times are simulated.
512 devices in a mesh: expert: 32 (over x_lo, z), tensor: 16 (over y, x_hi, core).
Axes of the slice: x: 4 (x_hi: 2, x_lo: 2; x = x_hi * 2 + x_lo), y: 4, z: 16, core: 2. Of those that a mesh axis runs over, the one named last changes fastest.
Arguments:
- tokens: bfloat16 [1536, 5120], P('expert', 'tensor'), may hold values from -6 to 6
- expert_ids: int32 [1536, 6], P('expert'), may hold values from 0 to 31, all different within a row; in each aligned block of 48 rows (0 to 47, 48 to 95, ...) at most 18 rows name the same one
- route_weights: float32 [1536, 6], P('expert'), may hold values from 0.05 to 0.6
- routed_gate: bfloat16 [32, 1536, 5120], P('expert', 'tensor'), may hold values from -0.078125 to 0.078125
- routed_up: bfloat16 [32, 1536, 5120], P('expert', 'tensor'), may hold values from -0.078125 to 0.078125
- routed_down: bfloat16 [32, 1536, 5120], P('expert', None, 'tensor'), may hold values from -0.15625 to 0.15625
- shared_gate: bfloat16 [5120, 3072], P('expert', 'tensor'), may hold values from -0.078125 to 0.078125
- shared_up: bfloat16 [5120, 3072], P('expert', 'tensor'), may hold values from -0.078125 to 0.078125
- shared_down: bfloat16 [3072, 5120], P('tensor', 'expert'), may hold values from -0.21875 to 0.21875
- norm_gain: float32 [5120], replicated, may hold values from 0.25 to 1.75
- proj_weight: bfloat16 [2112, 5120], P('tensor'), may hold values from -0.078125 to 0.078125
Outputs:
- stream: bfloat16 [1536, 5120], P('expert', 'tensor')
- projected: bfloat16 [1536, 2112], P('expert', 'tensor')
Inputs may be any that keep to these rules, and one draw needn't show every extreme that they name: `expert_ids`: in each aligned block of 48 tokens (those of one index of expert) no expert is chosen by more than 18 tokens, and some expert is chosen by exactly 18; a token's 6 experts differ.
All inputs are finite; a program needn't handle non-finite values.
Results may differ from a plain program's by a relative error of at most 0.019.
Values may be sent and summed in bfloat16 or wider, within the bound.
No kernel may reach another device: no remote copies, remote signals or barrier semaphores. Data moves between devices by JAX's collectives and lax.ppermute only.
A program may use at most 128 MiB of HBM per device.

v0:
```python
import jax
import jax.numpy as jnp
from jax import lax
from jax.sharding import PartitionSpec as P


def swiglu(gate, up):
    return (jax.nn.silu(gate) * up).astype(jnp.bfloat16)


def dot_rows(left, right):
    return lax.dot_general(
        left, right, (((1,), (1,)), ((), ())), preferred_element_type=jnp.float32
    )


def per_device(
    tokens,
    expert_ids,
    route_weights,
    routed_gate,
    routed_up,
    routed_down,
    shared_gate,
    shared_up,
    shared_down,
    norm_gain,
    proj_weight,
):
    tok_rows = tokens.shape[0]
    local_width = tokens.shape[1]
    top = expert_ids.shape[1]
    experts = lax.axis_size("expert")
    capacity = min(tok_rows, 2 * tok_rows * top // experts)
    features = lax.all_gather(tokens, "tensor", axis=1, tiled=True)
    flat_ids = expert_ids.reshape(-1)
    onehot = (flat_ids[:, None] == jnp.arange(experts, dtype=jnp.int32)[None, :]).astype(jnp.int32)
    slots = jnp.sum((jnp.cumsum(onehot, axis=0) - onehot) * onehot, axis=1)
    target = flat_ids * capacity + slots
    owners = jnp.repeat(jnp.arange(tok_rows, dtype=jnp.int32), top)
    sources = jnp.full((experts * capacity,), tok_rows, jnp.int32).at[target].set(owners)
    gate_w = routed_gate[0]
    up_w = routed_up[0]
    down_w = routed_down[0]
    padded = jnp.concatenate([features, jnp.zeros((1, features.shape[1]), features.dtype)], axis=0)
    outgoing = padded[sources].reshape(experts, capacity, features.shape[1])
    arrived = lax.all_to_all(outgoing, "expert", split_axis=0, concat_axis=0, tiled=True)
    count = arrived.shape[1]
    rows = arrived.reshape(-1, arrived.shape[2])
    hidden = swiglu(dot_rows(rows, gate_w), dot_rows(rows, up_w))
    hidden_all = lax.all_gather(hidden, "tensor", axis=1, tiled=True)
    result = jnp.dot(hidden_all, down_w, preferred_element_type=jnp.float32).astype(jnp.bfloat16)
    result = result.reshape(experts, count, result.shape[1])
    returned = lax.all_to_all(result, "expert", split_axis=0, concat_axis=0, tiled=True)
    flat_back = returned.reshape(experts * capacity, returned.shape[2])
    picked = flat_back[target].reshape(tok_rows, top, returned.shape[2]).astype(jnp.float32)
    routed = jnp.sum(picked * route_weights[:, :, None], axis=1)
    gate_sum = jnp.dot(
        features,
        lax.all_gather(shared_gate, "expert", axis=0, tiled=True),
        preferred_element_type=jnp.float32,
    )
    up_sum = jnp.dot(
        features,
        lax.all_gather(shared_up, "expert", axis=0, tiled=True),
        preferred_element_type=jnp.float32,
    )
    shared_hidden = swiglu(gate_sum, up_sum)
    shared_terms = jnp.dot(
        shared_hidden,
        lax.all_gather(shared_down, "expert", axis=1, tiled=True),
        preferred_element_type=jnp.float32,
    )
    rank = lax.axis_index("tensor")
    shared_full = lax.psum(shared_terms.astype(jnp.bfloat16), "tensor").astype(jnp.float32)
    shared_mine = lax.dynamic_slice_in_dim(shared_full, rank * local_width, local_width, 1)
    stream = (tokens.astype(jnp.float32) + shared_mine + routed).astype(jnp.bfloat16)
    stream_all = lax.all_gather(stream, "tensor", axis=1, tiled=True)
    values = stream_all.astype(jnp.float32)
    scale = lax.rsqrt(jnp.mean(values * values, axis=1, keepdims=True) + 1e-06)
    normed = (values * scale * norm_gain[None, :]).astype(jnp.bfloat16)
    projected = dot_rows(normed, proj_weight).astype(jnp.bfloat16)
    return (stream, projected)


def solution(mesh):
    in_specs = (
        P("expert", "tensor"),
        P("expert", None),
        P("expert", None),
        P("expert", "tensor", None),
        P("expert", "tensor", None),
        P("expert", None, "tensor"),
        P("expert", "tensor"),
        P("expert", "tensor"),
        P("tensor", "expert"),
        P(),
        P("tensor", None),
    )
    out_specs = (P("expert", "tensor"), P("expert", "tensor"))
    return jax.shard_map(
        per_device, mesh=mesh, in_specs=in_specs, out_specs=out_specs, check_vma=False
    )
```

profile of v0, /device:TPU:1, one launch (start us, length us, event | category | flops | bytes accessed | tf_op | source)
XLA Modules:
  0.0 1078.2 jit_solution(14754052590517255412)
XLA Ops:
  7.2 0.0 copy-start
  7.2 0.0 all-gather.13.cloned.1.call-start
  7.2 0.9 copy.26
  8.1 0.7 broadcast_multiply_fusion
  8.8 0.1 eq.22
  8.9 0.9 reduce-window.6
  9.8 0.2 slice_reduce_fusion
  10.1 0.1 bitcast_bitcast_fusion
  10.2 0.1 copy.25
  10.3 0.1 mul.68
  10.4 0.1 reshape.102
  10.6 2.9 scatter_custom_fusion
  13.5 29.4 %all-gather = bf16[16,320,48]{1,2,0:T(8,128)(2,1)S(1)} all-gather(bf16[1,320,48]{1,2,0:T(8,128)(2,1)} %bitcast.43), channel_id=1, replica_groups=mesh['expert'=32,'tensor'=16] {'tensor'}, dimensions={0}, use_global_device_ids=true | all-gather | bytes 522240 | tf_op jit(solution)/shard_map/all_gather | solution.py:35
  43.0 0.1 copy.24
  43.1 0.4 reshape.108
  43.6 6.0 gather_fusion
  49.6 8.5 reshape.76
  58.1 359.3 %all_to_all.10 = bf16[32,18,5120]{2,1,0:T(8,128)(2,1)} all-to-all(bf16[32,18,5120]{2,1,0:T(8,128)(2,1)} %reshape.76), channel_id=1, replica_groups=mesh['expert'=32,'tensor'=16] {'expert'}, dimensions={0} | all-to-all | bytes 11796480 | tf_op jit(solution)/shard_map/all_to_all | solution.py:47
  417.4 0.0 copy-start.2
  417.4 8.8 reshape.77
  426.2 0.0 copy-done.2
  426.2 0.0 copy-start.1
  426.2 4.8 fusion.4
  431.0 0.0 copy-done.1
  431.0 0.0 copy-done.6
  431.1 2.6 fusion
  433.7 0.0 all-gather.13.cloned.1.call-update
  433.7 0.0 all-gather.7.cloned.1.call-start
  433.8 0.7 all-gather.7.cloned.1.call-update
  434.5 0.0 all-gather.11.cloned.1.call-start
  434.5 0.7 all-gather.11.cloned.1.call-update
  435.2 0.0 all-gather.9.cloned.1.call-start
  435.3 0.5 all-gather.9.cloned.1.call-update
  435.8 51.4 %all-gather.13.cloned.1.call-done = bf16[576,1536]{0,1:T(8,128)(2,1)} async-done(((bf16[576,96]{0,1:T(8,128)(2,1)}), bf16[576,1536]{0,1:T(8,128)(2,1)}) %all-gather.13.cloned.1.call-update) | async-done | bytes 1769488 | tf_op jit(solution)/shard_map/all_gather | solution.py:51
  487.2 2.8 convolution_convert_fusion.1
  490.0 0.2 copy.29
  490.2 1.0 reshape.78
  491.3 12.3 %all-to-all-start.1 = ((bf16[32,18,320]{2,1,0:T(8,128)(2,1)}), bf16[32,18,320]{2,1,0:T(8,128)(2,1)S(1)}, u32[]{:S(2)}, u32[]{:S(2)}) async-start(bf16[32,18,320]{2,1,0:T(8,128)(2,1)} %reshape.78), calls=%async_computation.1 | async-start | bytes 1179648 | tf_op jit(solution)/shard_map/all_to_all | solution.py:54
  503.6 0.2 all-reduce.4.cloned.1.call-start
  503.8 110.9 %all-gather.7.cloned.1.call-done = bf16[5120,192]{1,0:T(8,128)(2,1)} async-done(((bf16[160,192]{1,0:T(8,128)(2,1)}), bf16[5120,192]{1,0:T(8,128)(2,1)}) %all-gather.7.cloned.1.call-update) | async-done | bytes 1966096 | tf_op jit(solution)/shard_map/all_gather | solution.py:60
  614.7 2.3 fusion.20
  617.0 0.0 copy-start.5
  617.0 123.6 %all-gather.11.cloned.1.call-done = bf16[192,5120]{0,1:T(8,128)(2,1)} async-done(((bf16[192,160]{0,1:T(8,128)(2,1)}), bf16[192,5120]{0,1:T(8,128)(2,1)}) %all-gather.11.cloned.1.call-update) | async-done | bytes 1966096 | tf_op jit(solution)/shard_map/all_gather | solution.py:71
  740.7 130.1 %all-gather.9.cloned.1.call-done = bf16[5120,192]{1,0:T(8,128)(2,1)} async-done(((bf16[160,192]{1,0:T(8,128)(2,1)}), bf16[5120,192]{1,0:T(8,128)(2,1)}) %all-gather.9.cloned.1.call-update) | async-done | bytes 1966096 | tf_op jit(solution)/shard_map/all_gather | solution.py:65
  870.8 5.2 convolution_convert_fusion
  876.0 0.0 all-reduce.4.cloned.1.call-update
  876.0 0.0 copy-done.5
  876.0 0.1 copy.30
  876.1 0.0 all-to-all-done.1
  876.1 0.2 reshape.79
  876.4 2.0 gather_fusion.1
  878.4 0.1 reshape.81
  878.4 0.2 multiply_reduce_fusion.1
  878.7 161.6 %all-reduce.4.cloned.1.call-done = bf16[48,5120]{1,0:T(8,128)(2,1)} async-done(((bf16[48,5120]{1,0:T(8,128)(2,1)}), bf16[48,5120]{1,0:T(8,128)(2,1)}) %all-reduce.4.cloned.1.call-update) | async-done | bytes 491536 | tf_op jit(solution)/shard_map/psum | solution.py:75
  1040.3 0.0 copy-done.3
  1040.3 0.9 add_convert_fusion
  1041.2 0.0 copy-start.4
  1041.2 27.8 %all-gather.1 = bf16[16,320,48]{1,2,0:T(8,128)(2,1)S(1)} all-gather(bf16[1,320,48]{1,2,0:T(8,128)(2,1)S(1)} %bitcast.44), channel_id=1, replica_groups=mesh['expert'=32,'tensor'=16] {'tensor'}, dimensions={0}, use_global_device_ids=true | all-gather | bytes 522240 | tf_op jit(solution)/shard_map/all_gather | solution.py:78
  1069.0 0.0 copy-done.4
  1069.0 0.1 copy.31
  1069.1 0.3 reshape.111
  1069.5 0.2 multiply_reduce_fusion
  1069.7 0.0 copy-done
  1069.7 2.0 convolution_convert_fusion.2
  (13 shorter events, 0.2 us)
Async XLA Ops:
  7.2 1062.5 %copy-start = (bf16[132,5120]{1,0:T(8,128)(2,1)S(1)}, bf16[132,5120]{1,0:T(8,128)(2,1)}, u32[]{:S(2)}) copy-start(bf16[132,5120]{1,0:T(8,128)(2,1)} %param.21) | copy-start | bytes 4055044
  7.2 480.0 %all-gather.13.cloned.1.call-start = ((), (), s32[]{:S(2)}) async-start(), calls=%async_computation.6 | async-start | bytes 2088960 | tf_op jit(solution)/shard_map/all_gather | solution.py:51
  417.4 8.8 copy-start.2
  426.2 4.8 copy-start.1
  426.2 4.8 copy-start.6
  433.7 181.0 %all-gather.7.cloned.1.call-start = ((), (), s32[]{:S(2)}) async-start(), calls=%async_computation.2 | async-start | bytes 2703360 | tf_op jit(solution)/shard_map/all_gather | solution.py:60
  434.5 306.2 %all-gather.11.cloned.1.call-start = ((), (), s32[]{:S(2)}) async-start(), calls=%async_computation.4 | async-start | bytes 2703360 | tf_op jit(solution)/shard_map/all_gather | solution.py:71
  435.2 435.6 %all-gather.9.cloned.1.call-start = ((), (), s32[]{:S(2)}) async-start(), calls=%async_computation.3 | async-start | bytes 2703360 | tf_op jit(solution)/shard_map/all_gather | solution.py:65
  491.3 384.9 %all-to-all-start.1 = ((bf16[32,18,320]{2,1,0:T(8,128)(2,1)}), bf16[32,18,320]{2,1,0:T(8,128)(2,1)S(1)}, u32[]{:S(2)}, u32[]{:S(2)}) async-start(bf16[32,18,320]{2,1,0:T(8,128)(2,1)} %reshape.78), calls=%async_computation.1 | async-start | bytes 1179648 | tf_op jit(solution)/shard_map/all_to_all | solution.py:54
  503.6 536.8 %all-reduce.4.cloned.1.call-start = ((), (), s32[]{:S(2)}) async-start(), calls=%async_computation.5 | async-start | bytes 983040 | tf_op jit(solution)/shard_map/psum | solution.py:75
  617.0 259.0 %copy-start.5 = (f32[48,6]{0,1:T(8,128)S(1)}, f32[48,6]{0,1:T(8,128)}, u32[]{:S(2)}) copy-start(f32[48,6]{0,1:T(8,128)} %param.13) | copy-start | bytes 3460
  876.0 164.4 %copy-start.3 = (bf16[48,320]{1,0:T(8,128)(2,1)S(1)}, bf16[48,320]{1,0:T(8,128)(2,1)}, u32[]{:S(2)}) copy-start(bf16[48,320]{1,0:T(8,128)(2,1)} %param.11) | copy-start | bytes 92164
  1041.2 27.8 %copy-start.4 = (bf16[48,320]{1,0:T(8,128)(2,1)}, bf16[48,320]{1,0:T(8,128)(2,1)S(1)}, u32[]{:S(2)}) copy-start(bf16[48,320]{1,0:T(8,128)(2,1)S(1)} %add_convert_fusion) | copy-start | bytes 92164
Sparse Core Ops, SparseCore 0:
  433.8 53.3 all-gather.12
  489.3 125.3 all-gather.6
  616.8 123.8 all-gather.10
  742.6 128.1 all-gather.8
  876.1 164.1 all-reduce.3
where the time goes:
time: 1080 us
  waiting for transfers between devices  580 us (54%)
  blocking collectives  416 us (39%)
  local copies, waits for them, and re-layouts  32.6 us (3%)
  matrix products  19.7 us (2%)
  between operations  14 us (1%)
  starting transfers between devices  12.7 us (1%)
    all_to_all x1, blocking collectives, per_device(): lax.all_to_all(outgoing, 'expert', split_axis=0, concat_axis=0, tiled=True)  359 us
    psum x1, waiting for transfers between devices, per_device(): lax.psum(shared_terms.astype(jnp.bfloat16), 'tensor').astype(jnp.float32)  162 us
    all_gather x1, waiting for transfers between devices, per_device(): lax.all_gather(shared_up, 'expert', axis=0, tiled=True)  130 us
    all_gather x1, waiting for transfers between devices, per_device(): lax.all_gather(shared_down, 'expert', axis=1, tiled=True)  124 us
    all_gather x1, waiting for transfers between devices, per_device(): lax.all_gather(shared_gate, 'expert', axis=0, tiled=True)  111 us
    all_gather x1, waiting for transfers between devices, per_device(): hidden_all = lax.all_gather(hidden, 'tensor', axis=1, tiled=True)  51.4 us
    all_gather x1, blocking collectives, per_device(): features = lax.all_gather(tokens, 'tensor', axis=1, tiled=True)  29.4 us
    all_gather x1, blocking collectives, per_device(): stream_all = lax.all_gather(stream, 'tensor', axis=1, tiled=True)  27.8 us
  transfers between devices with their start and end apart: 6, of which 5 were waited for; matrix products, arithmetic and copies ran while one was open for 1% of the time, Pallas kernels for 0%

commit v1 on v0

--- a/solution.py
+++ b/solution.py
@@ -2,6 +2,11 @@
 import jax.numpy as jnp
 from jax import lax
 from jax.sharding import PartitionSpec as P
+
+
+def swapped_in(value, axis, dim):
+    sent = jnp.stack([value] * lax.axis_size(axis))
+    return jnp.concatenate(lax.all_to_all(sent, axis, 0, 0), axis=dim)
 
 
 def swiglu(gate, up):
@@ -56,9 +61,7 @@
     picked = flat_back[target].reshape(tok_rows, top, returned.shape[2]).astype(jnp.float32)
     routed = jnp.sum(picked * route_weights[:, :, None], axis=1)
     gate_sum = jnp.dot(
-        features,
-        lax.all_gather(shared_gate, "expert", axis=0, tiled=True),
-        preferred_element_type=jnp.float32,
+        features, swapped_in(shared_gate, "expert", 0), preferred_element_type=jnp.float32
     )
     up_sum = jnp.dot(
         features,

time: 1080 us -> 974 us (0.902)
  waiting for transfers between devices: 580 us -> 467 us
    all_gather x1 -> x0, waiting for transfers between devices: 111 us -> none  [per_device(): lax.all_gather(shared_gate, 'expert', axis=0, tiled=True)]
    all_to_all x0 -> x1, waiting for transfers between devices: none -> 73 us  [swapped_in(): return jnp.concatenate(lax.all_to_all(sent, axis, 0, 0), axis=dim)]
    all_gather x1, waiting for transfers between devices: 130 us -> 65.8 us  [per_device(): lax.all_gather(shared_up, 'expert', axis=0, tiled=True)]
  transfers between devices with their start and end apart: 6 -> 6, of which waited for: 5 -> 5; matrix products, arithmetic and copies ran while one was open for 1% -> 2% of each run, Pallas kernels for 0% -> 0%
where the time goes in v1:
time: 974 us; the launch traced here: 973 us
  waiting for transfers between devices  467 us (48%)
  blocking collectives  416 us (43%)
  local copies, waits for them, and re-layouts  34.4 us (4%)
  matrix products  19.7 us (2%)
  starting transfers between devices  18.1 us (2%)
  between operations  14 us (1%)
    all_to_all x1, blocking collectives, per_device(): lax.all_to_all(outgoing, 'expert', split_axis=0, concat_axis=0, tiled=True)  359 us
    psum x1, waiting for transfers between devices, per_device(): lax.psum(shared_terms.astype(jnp.bfloat16), 'tensor').astype(jnp.float32)  162 us
    all_gather x1, waiting for transfers between devices, per_device(): lax.all_gather(shared_down, 'expert', axis=1, tiled=True)  121 us
    all_to_all x1, waiting for transfers between devices, swapped_in(): return jnp.concatenate(lax.all_to_all(sent, axis, 0, 0), axis=dim)  73 us
    all_gather x1, waiting for transfers between devices, per_device(): lax.all_gather(shared_up, 'expert', axis=0, tiled=True)  65.8 us
    all_gather x1, waiting for transfers between devices, per_device(): hidden_all = lax.all_gather(hidden, 'tensor', axis=1, tiled=True)  44.8 us
    all_gather x1, blocking collectives, per_device(): features = lax.all_gather(tokens, 'tensor', axis=1, tiled=True)  29.4 us
    all_gather x1, blocking collectives, per_device(): stream_all = lax.all_gather(stream, 'tensor', axis=1, tiled=True)  27.8 us
  transfers between devices with their start and end apart: 6, of which 5 were waited for; matrix products, arithmetic and copies ran while one was open for 2% of the time, Pallas kernels for 0%

profile of v1, /device:TPU:1, one launch (start us, length us, event | category | flops | bytes accessed | tf_op | source)
XLA Modules:
  0.0 973.3 jit_solution(8107992231485424440)
XLA Ops:
  7.2 0.0 copy-start
  7.2 0.0 all-gather.10.cloned.1.call-start
  7.2 0.9 copy.26
  8.1 0.7 broadcast_multiply_fusion
  8.8 0.1 eq.22
  8.9 0.9 reduce-window.6
  9.8 0.2 slice_reduce_fusion
  10.1 0.1 bitcast_bitcast_fusion
  10.2 0.1 copy.25
  10.3 0.1 mul.68
  10.4 0.1 reshape.108
  10.6 2.9 scatter_custom_fusion
  13.5 29.4 %all-gather = bf16[16,320,48]{1,2,0:T(8,128)(2,1)S(1)} all-gather(bf16[1,320,48]{1,2,0:T(8,128)(2,1)} %bitcast.44), channel_id=1, replica_groups=mesh['expert'=32,'tensor'=16] {'tensor'}, dimensions={0}, use_global_device_ids=true | all-gather | bytes 522240 | tf_op jit(solution)/shard_map/all_gather | solution.py:40
  43.0 0.1 copy.24
  43.1 0.4 reshape.114
  43.6 6.0 gather_fusion
  49.6 8.5 reshape.82
  58.1 359.3 %all_to_all.15 = bf16[32,18,5120]{2,1,0:T(8,128)(2,1)} all-to-all(bf16[32,18,5120]{2,1,0:T(8,128)(2,1)} %reshape.82), channel_id=1, replica_groups=mesh['expert'=32,'tensor'=16] {'expert'}, dimensions={0} | all-to-all | bytes 11796480 | tf_op jit(solution)/shard_map/all_to_all | solution.py:52
  417.4 8.8 reshape.83
  426.2 0.0 copy-done.2
  426.2 4.8 fusion.4
  431.0 0.0 copy-done.1
  431.0 0.0 copy-done.7
  431.1 0.0 copy-start.5
  431.1 2.7 fusion
  433.7 0.0 all-gather.10.cloned.1.call-update
  433.7 0.0 copy-done.5
  433.8 1.9 stack.2
  435.6 6.5 all-to-all-start
  442.1 0.0 all-gather.6.cloned.1.call-start
  442.1 0.7 all-gather.6.cloned.1.call-update
  442.8 0.0 all-gather.8.cloned.1.call-start
  442.9 0.7 all-gather.8.cloned.1.call-update
  443.6 44.8 %all-gather.10.cloned.1.call-done = bf16[576,1536]{0,1:T(8,128)(2,1)} async-done(((bf16[576,96]{0,1:T(8,128)(2,1)}), bf16[576,1536]{0,1:T(8,128)(2,1)}) %all-gather.10.cloned.1.call-update) | async-done | bytes 1769488 | tf_op jit(solution)/shard_map/all_gather | solution.py:56
  488.4 2.8 convolution_convert_fusion.1
  491.2 0.2 copy.29
  491.4 1.0 reshape.84
  492.4 73.0 %all-to-all-done = bf16[32,160,192]{2,1,0:T(8,128)(2,1)} async-done(((bf16[32,160,192]{2,1,0:T(8,128)(2,1)}), bf16[32,160,192]{2,1,0:T(8,128)(2,1)}, u32[]{:S(2)}, u32[]{:S(2)}) %all-to-all-start) | async-done | bytes 1966112 | tf_op jit(solution)/shard_map/all_to_all | solution.py:9
  565.4 11.3 %all-to-all-start.2 = ((bf16[32,18,320]{2,1,0:T(8,128)(2,1)}), bf16[32,18,320]{2,1,0:T(8,128)(2,1)S(1)}, u32[]{:S(2)}, u32[]{:S(2)}) async-start(bf16[32,18,320]{2,1,0:T(8,128)(2,1)} %reshape.84), calls=%async_computation.2 | async-start | bytes 1179648 | tf_op jit(solution)/shard_map/all_to_all | solution.py:59
  576.7 0.2 all-reduce.4.cloned.1.call-start
  576.9 2.3 fusion.20
  579.3 0.0 copy-start.6
  579.3 65.8 %all-gather.6.cloned.1.call-done = bf16[5120,192]{1,0:T(8,128)(2,1)} async-done(((bf16[160,192]{1,0:T(8,128)(2,1)}), bf16[5120,192]{1,0:T(8,128)(2,1)}) %all-gather.6.cloned.1.call-update) | async-done | bytes 1966096 | tf_op jit(solution)/shard_map/all_gather | solution.py:68
  645.1 120.8 %all-gather.8.cloned.1.call-done = bf16[192,5120]{0,1:T(8,128)(2,1)} async-done(((bf16[192,160]{0,1:T(8,128)(2,1)}), bf16[192,5120]{0,1:T(8,128)(2,1)}) %all-gather.8.cloned.1.call-update) | async-done | bytes 1966096 | tf_op jit(solution)/shard_map/all_gather | solution.py:74
  765.9 5.2 convolution_convert_fusion
  771.1 0.0 all-reduce.4.cloned.1.call-update
  771.1 0.0 copy-done.6
  771.1 0.1 copy.30
  771.2 0.0 all-to-all-done.2
  771.3 0.2 reshape.85
  771.5 2.0 gather_fusion.1
  773.5 0.1 reshape.87
  773.6 0.2 multiply_reduce_fusion.1
  773.8 161.6 %all-reduce.4.cloned.1.call-done = bf16[48,5120]{1,0:T(8,128)(2,1)} async-done(((bf16[48,5120]{1,0:T(8,128)(2,1)}), bf16[48,5120]{1,0:T(8,128)(2,1)}) %all-reduce.4.cloned.1.call-update) | async-done | bytes 491536 | tf_op jit(solution)/shard_map/psum | solution.py:78
  935.5 0.0 copy-done.3
  935.5 0.9 add_convert_fusion
  936.3 0.0 copy-start.4
  936.4 27.8 %all-gather.1 = bf16[16,320,48]{1,2,0:T(8,128)(2,1)S(1)} all-gather(bf16[1,320,48]{1,2,0:T(8,128)(2,1)S(1)} %bitcast.45), channel_id=1, replica_groups=mesh['expert'=32,'tensor'=16] {'tensor'}, dimensions={0}, use_global_device_ids=true | all-gather | bytes 522240 | tf_op jit(solution)/shard_map/all_gather | solution.py:81
  964.1 0.0 copy-done.4
  964.1 0.1 copy.31
  964.3 0.3 reshape.117
  964.6 0.2 multiply_reduce_fusion
  964.8 0.0 copy-done
  964.8 2.0 convolution_convert_fusion.2
  (15 shorter events, 0.2 us)
Async XLA Ops:
  7.2 957.6 %copy-start = (bf16[132,5120]{1,0:T(8,128)(2,1)S(1)}, bf16[132,5120]{1,0:T(8,128)(2,1)}, u32[]{:S(2)}) copy-start(bf16[132,5120]{1,0:T(8,128)(2,1)} %param.21) | copy-start | bytes 4055044
  7.2 481.2 %all-gather.10.cloned.1.call-start = ((), (), s32[]{:S(2)}) async-start(), calls=%async_computation.6 | async-start | bytes 2088960 | tf_op jit(solution)/shard_map/all_gather | solution.py:56
  417.4 8.8 copy-start.2
  426.2 4.8 copy-start.1
  426.2 4.8 copy-start.7
  431.1 2.7 copy-start.5
  435.6 129.8 %all-to-all-start = ((bf16[32,160,192]{2,1,0:T(8,128)(2,1)}), bf16[32,160,192]{2,1,0:T(8,128)(2,1)}, u32[]{:S(2)}, u32[]{:S(2)}) async-start(bf16[32,160,192]{2,1,0:T(8,128)(2,1)} %stack.2), calls=%async_computation | async-start | bytes 5242880 | tf_op jit(solution)/shard_map/all_to_all | solution.py:9
  442.1 203.0 %all-gather.6.cloned.1.call-start = ((), (), s32[]{:S(2)}) async-start(), calls=%async_computation.3 | async-start | bytes 2703360 | tf_op jit(solution)/shard_map/all_gather | solution.py:68
  442.8 323.0 %all-gather.8.cloned.1.call-start = ((), (), s32[]{:S(2)}) async-start(), calls=%async_computation.4 | async-start | bytes 2703360 | tf_op jit(solution)/shard_map/all_gather | solution.py:74
  565.4 205.9 %all-to-all-start.2 = ((bf16[32,18,320]{2,1,0:T(8,128)(2,1)}), bf16[32,18,320]{2,1,0:T(8,128)(2,1)S(1)}, u32[]{:S(2)}, u32[]{:S(2)}) async-start(bf16[32,18,320]{2,1,0:T(8,128)(2,1)} %reshape.84), calls=%async_computation.2 | async-start | bytes 1179648 | tf_op jit(solution)/shard_map/all_to_all | solution.py:59
  576.7 358.7 %all-reduce.4.cloned.1.call-start = ((), (), s32[]{:S(2)}) async-start(), calls=%async_computation.5 | async-start | bytes 983040 | tf_op jit(solution)/shard_map/psum | solution.py:78
  579.3 191.9 %copy-start.6 = (f32[48,6]{0,1:T(8,128)S(1)}, f32[48,6]{0,1:T(8,128)}, u32[]{:S(2)}) copy-start(f32[48,6]{0,1:T(8,128)} %param.13) | copy-start | bytes 3460
  771.1 164.4 %copy-start.3 = (bf16[48,320]{1,0:T(8,128)(2,1)S(1)}, bf16[48,320]{1,0:T(8,128)(2,1)}, u32[]{:S(2)}) copy-start(bf16[48,320]{1,0:T(8,128)(2,1)} %param.11) | copy-start | bytes 92164
  936.3 27.8 %copy-start.4 = (bf16[48,320]{1,0:T(8,128)(2,1)}, bf16[48,320]{1,0:T(8,128)(2,1)S(1)}, u32[]{:S(2)}) copy-start(bf16[48,320]{1,0:T(8,128)(2,1)S(1)} %add_convert_fusion) | copy-start | bytes 92164
Sparse Core Ops, SparseCore 0:
  433.9 54.4 all-gather.9
  490.5 154.5 all-gather.5
  647.2 118.6 all-gather.7
  771.3 164.1 all-reduce.3
